TPU v7x, 256 devices: a whole 4x4x8 slice. The times are simulated.
256 devices in a mesh: rep: 8 (over x, core), fsdp: 32 (over y, z).
Axes of the slice: x: 4, y: 4, z: 8, core: 2. Of those that a mesh axis runs over, the one named last changes fastest.
Arguments:
- tokens: bfloat16 [65536, 4608], P(('rep', 'fsdp')), may hold values from -24 to 24
- cotangent: bfloat16 [65536, 1024], P(('rep', 'fsdp')), may hold values from -0.0625 to 0.0625
- weight: bfloat16 [4608, 1024], P('fsdp'), may hold values from -0.09375 to 0.09375
- momentum: float32 [8, 4608, 1024], P('rep', 'fsdp'), may hold values from -6 to 6
- lengths: int32 [256], P(('rep', 'fsdp')), may hold values from 1 to 256, as said below
- kept_index: int32 [4608, 256], P('fsdp'), may hold values from 0 to 31, as said below
Outputs:
- projected: bfloat16 [65536, 1024], P(('rep', 'fsdp'))
- new_momentum: float32 [8, 4608, 1024], P('rep', 'fsdp')
- update: float32 [4608, 1024], P('fsdp')
Inputs may be any that keep to these rules, and one draw needn't show every extreme that they name: `lengths`: some sample has exactly 256 live tokens. `kept_index`: the 16 indices of one piece are distinct.
All inputs are finite; a program needn't handle non-finite values.
Results may differ from a plain program's by a relative error of at most 0.014.
Values may be sent and summed in bfloat16 or wider, within the bound.
No kernel may reach another device: no remote copies, remote signals or barrier semaphores. Data moves between devices by JAX's collectives and lax.ppermute only.
A program may use at most 128 MiB of HBM per device.

v0:
```python
import jax
import jax.numpy as jnp
from jax import lax
from jax.sharding import PartitionSpec as P

PIECE = 64
TOPK = 16
SLOT = 256


def dct_matrix():
    frequency = lax.broadcasted_iota(jnp.int32, (PIECE, PIECE), 0).astype(jnp.float32)
    position = lax.broadcasted_iota(jnp.int32, (PIECE, PIECE), 1).astype(jnp.float32)
    norm_scale = jnp.where(frequency == 0.0, jnp.sqrt(1.0 / PIECE), jnp.sqrt(2.0 / PIECE))
    return norm_scale * jnp.cos(jnp.pi * (2.0 * position + 1.0) * frequency / (2.0 * PIECE))


def contract_rows(left, right):
    return lax.dot_general(
        left, right, (((0,), (0,)), ((), ())), preferred_element_type=jnp.float32
    )


def per_device(tokens, cotangent, weight, momentum, lengths, kept_index):
    num_rep = lax.axis_size("rep")
    tok_rows = tokens.shape[0]
    kv_width = weight.shape[1]
    local_rows = weight.shape[0]
    highest = lax.Precision.HIGHEST
    columns = tokens
    summed = jnp.dot(
        columns,
        lax.all_gather(weight, "fsdp", axis=0, tiled=True),
        preferred_element_type=jnp.float32,
    )
    projected = summed.astype(jnp.bfloat16)
    sample_count = lengths.shape[0]
    live_mask = lax.broadcasted_iota(jnp.int32, (sample_count, SLOT), 1) < lengths[:, None]
    masked = cotangent.reshape(sample_count, SLOT, kv_width) * live_mask[:, :, None].astype(
        jnp.bfloat16
    )
    masked = masked.reshape(tok_rows, kv_width)
    columns = tokens
    grad = lax.psum_scatter(
        contract_rows(columns, masked).astype(jnp.bfloat16), "fsdp", scatter_dimension=0, tiled=True
    ).astype(jnp.float32)
    blended = 0.9 * momentum[0] + grad
    dct_table = dct_matrix()
    pair_table = jnp.kron(jnp.eye(128 // PIECE, dtype=jnp.float32), dct_table)
    pairs = kv_width // 128
    pieces = kv_width // PIECE
    coeffs = jnp.einsum(
        "rpn,kn->rpk", blended.reshape(local_rows, pairs, 128), pair_table, precision=highest
    )
    coeffs = coeffs.reshape(local_rows, pieces, PIECE)
    kept = kept_index.reshape(local_rows, pieces, TOPK)
    selector = (kept[:, :, :, None] == lax.broadcasted_iota(jnp.int32, (1, 1, 1, PIECE), 3)).astype(
        jnp.float32
    )
    values = jnp.einsum("rpk,rpjk->rpj", coeffs, selector, precision=highest)
    dense_coeffs = jnp.einsum("rpj,rpjk->rpk", values, selector, precision=highest)
    rebuilt_pairs = jnp.einsum(
        "rpk,kn->rpn", dense_coeffs.reshape(local_rows, pairs, 128), pair_table, precision=highest
    )
    new_momentum = (blended - rebuilt_pairs.reshape(local_rows, kv_width))[None]
    every_group = lax.all_gather(
        values.reshape(1, local_rows, pieces * TOPK), "rep", axis=0, tiled=True
    )
    every_group = every_group.reshape(num_rep, local_rows, pieces, TOPK)
    dense_every = jnp.einsum("grpj,rpjk->grpk", every_group, selector, precision=highest)
    rebuilt_every = jnp.einsum(
        "grpk,kn->grpn",
        dense_every.reshape(num_rep, local_rows, pairs, 128),
        pair_table,
        precision=highest,
    )
    update = jnp.sum(rebuilt_every.reshape(num_rep, local_rows, kv_width), axis=0)
    return (projected, new_momentum, update)


def solution(mesh):
    placed = (
        P(("rep", "fsdp"), None),
        P(("rep", "fsdp"), None),
        P("fsdp", None),
        P("rep", "fsdp", None),
        P(("rep", "fsdp")),
        P("fsdp", None),
    )
    return jax.shard_map(
        per_device,
        mesh=mesh,
        in_specs=placed,
        out_specs=(P(("rep", "fsdp"), None), P("rep", "fsdp", None), P("fsdp", None)),
        check_vma=False,
    )
```

profile of v0, /device:TPU:1, one launch (start us, length us, event | category | flops | bytes accessed | tf_op | source)
XLA Modules:
  0.0 451.7 jit_solution(8315757887169938571)
XLA Ops:
  8.9 6.4 %fusion.6 = bf16[4608,1024]{0,1:T(8,128)(2,1)} fusion(bf16[256,4608]{1,0:T(8,128)(2,1)S(1)} %copy-done, bf16[256,1024]{1,0:T(8,128)(2,1)} %param.7, bf16[256]{0:T(256)(128)(2,1)S(1)} %compare_convert_fusion.1), kind=kOutput, calls=%fused_computation.8 | convolution fusion | flops 2420899840 | bytes 12321280 | tf_op jit(solution)/shard_map/dot_general | solution.py:19
  15.2 12.6 %copy.37 = bf16[4608,1024]{1,0:T(8,128)(2,1)} copy(bf16[4608,1024]{0,1:T(8,128)(2,1)} %fusion.6) | data formatting | bytes 18874368
  29.8 1.3 copy.21
  31.3 1.5 copy.24
  32.7 227.4 %reduce-scatter.4.cloned.1.call-done = bf16[144,1024]{1,0:T(8,128)(2,1)} async-done(((bf16[4608,1024]{1,0:T(8,128)(2,1)}), bf16[144,1024]{1,0:T(8,128)(2,1)}) %reduce-scatter.4.cloned.1.call-update) | async-done | bytes 294928
  260.2 2.0 copy.38
  262.1 1.5 bitcast_add_fusion
  263.7 1.2 copy.22
  264.8 2.5 fusion.11
  267.3 2.3 reshape.123
  269.6 19.0 %fusion.2 = f32[144,16,1,16]{3,2,1,0:T(1,128)} fusion(f32[144,16,64,1]{2,3,1,0:T(1,128)} %bitcast.48, s32[144,16,16]{2,1,0:T(8,128)} %copy.24), kind=kOutput, calls=%fused_computation.3 | convolution fusion | flops 30670848 | bytes 884736 | tf_op jit(solution)/shard_map/rpk,rpjk->rpj/dot_general | solution.py:60
  288.7 3.6 copy.32
  292.2 1.7 copy.26
  294.7 73.6 %all-gather.3.cloned.1.call-done = bf16[4608,1024]{1,0:T(8,128)(2,1)} async-done(((bf16[144,1024]{1,0:T(8,128)(2,1)}), bf16[4608,1024]{1,0:T(8,128)(2,1)}) %all-gather.3.cloned.1.call-update) | async-done | bytes 9437200 | tf_op jit(solution)/shard_map/all_gather | solution.py:33
  368.3 7.1 %convolution_convert_fusion.1 = bf16[256,1024]{1,0:T(8,128)(2,1)} fusion(bf16[256,4608]{1,0:T(8,128)(2,1)S(1)} %copy-done, bf16[4608,1024]{1,0:T(8,128)(2,1)} %all-gather.3.cloned.1.call-done), kind=kOutput, calls=%fused_computation.11 | convolution fusion | flops 2416181248 | bytes 12320768 | tf_op jit(solution)/shard_map/dot_general | solution.py:31
  375.4 2.3 copy.33
  377.6 15.8 %fusion.1 = f32[144,16,1,64]{3,2,1,0:T(1,128)S(1)} fusion(f32[144,16,16,1]{2,3,1,0:T(1,128)S(1)} %copy.33, s32[144,16,16]{2,1,0:T(8,128)} %copy.24), kind=kOutput, calls=%fused_computation.2 | convolution fusion | flops 30670848 | bytes 884736 | tf_op jit(solution)/shard_map/rpj,rpjk->rpk/dot_general | solution.py:61
  394.8 1.1 copy.30
  395.9 1.8 copy.27
  397.7 8.5 %copy.28 = f32[8,144,16,16]{3,0,2,1:T(8,128)} copy(f32[8,144,16,16]{1,3,2,0:T(8,128)S(1)} %bitcast.43) | data formatting | bytes 2359296 | tf_op jit(solution)/shard_map/reshape | solution.py:69
  406.2 18.0 %fusion.7 = f32[8,144,16,64]{3,0,2,1:T(8,128)S(1)} fusion(f32[8,144,16,16]{3,0,2,1:T(8,128)} %copy.28, s32[144,16,16]{2,1,0:T(8,128)S(1)} %copy-done.2), kind=kOutput, calls=%fused_computation.9 | convolution fusion | flops 228851712 | bytes 6045696 | tf_op jit(solution)/shard_map/grpj,rpjk->grpk/dot_general | solution.py:70
  424.2 5.3 %copy.29 = f32[8,144,16,64]{3,2,1,0:T(8,128)} copy(f32[8,144,16,64]{3,0,2,1:T(8,128)S(1)} %fusion.7) | data formatting | bytes 9437184 | tf_op jit(solution)/shard_map/grpj,rpjk->grpk/transpose | solution.py:70
  429.6 8.9 %reshape.121 = f32[8,144,8,128]{3,2,1,0:T(8,128)} reshape(f32[8,144,16,64]{3,2,1,0:T(8,128)} %copy.29) | data formatting | bytes 9437184 | tf_op jit(solution)/shard_map/reshape | solution.py:73
  438.5 5.7 %convolution_reduce_fusion = f32[144,8,128]{2,1,0:T(8,128)S(1)} fusion(f32[8,144,8,128]{3,2,1,0:T(8,128)} %reshape.121, f32[128,128,1,1]{1,0,2,3:T(8,128)S(1)} %copy-done.5), kind=kOutput, calls=%fused_computation.10 | convolution fusion | flops 1812971520 | bytes 5373952 | tf_op jit(solution)/shard_map/grpk,kn->grpn/dot_general | solution.py:71
  (35 shorter events, 5.9 us)
Async XLA Ops:
  7.2 1.7 copy-start
  7.2 253.0 %reduce-scatter.4.cloned.1.call-start = ((), (), s32[]{:S(2)}) async-start(), calls=%async_computation.3 | async-start | bytes 9732096
  27.9 1.9 copy-start.3
  27.9 3.3 copy-start.6
  27.9 340.4 %all-gather.3.cloned.1.call-start = ((), (), s32[]{:S(2)}) async-start(), calls=%async_computation.1 | async-start | bytes 9732096 | tf_op jit(solution)/shard_map/all_gather | solution.py:33
  28.6 367.2 %all-gather.5.cloned.1.call-start = ((), (), s32[]{:S(2)}) async-start(), calls=%async_computation.2 | async-start | bytes 1327104 | tf_op jit(solution)/shard_map/all_gather | solution.py:66
  377.6 16.0 %copy-start.4 = (f32[128,128,1]{1,0,2:T(8,128)S(1)}, f32[128,128,1]{1,0,2:T(8,128)}, u32[]{:S(2)}) copy-start(f32[128,128,1]{1,0,2:T(8,128)} %reshape.122) | copy-start | bytes 196612
  397.7 8.5 %copy-start.2 = (s32[144,16,16]{2,1,0:T(8,128)S(1)}, s32[144,16,16]{2,1,0:T(8,128)}, u32[]{:S(2)}) copy-start(s32[144,16,16]{2,1,0:T(8,128)} %copy.24) | copy-start | bytes 442372
  429.6 8.9 %copy-start.5 = (f32[128,128,1,1]{1,0,2,3:T(8,128)S(1)}, f32[128,128,1,1]{1,0,2,3:T(8,128)}, u32[]{:S(2)}) copy-start(f32[128,128,1,1]{1,0,2,3:T(8,128)} %reshape.127) | copy-start | bytes 196612
  429.6 15.5 %copy-start.1 = (bf16[256,4608]{1,0:T(8,128)(2,1)S(1)}, bf16[256,4608]{1,0:T(8,128)(2,1)}, u32[]{:S(2)}) copy-start(bf16[256,4608]{1,0:T(8,128)(2,1)} %param.6) | copy-start | bytes 7077892
Sparse Core Ops, SparseCore 0:
  28.0 232.1 reduce-scatter.3
  262.7 105.4 all-gather.2
  370.1 24.0 all-gather.4
where the time goes:
time: 453 us; the launch traced here: 452 us
  waiting for transfers between devices  302 us (67%)
  matrix products  75.1 us (17%)
  local copies, waits for them, and re-layouts  58 us (13%)
  between operations  14.7 us (3%)
    unnamed x4, waiting for transfers between devices  228 us
    all_gather x1, waiting for transfers between devices, per_device(): lax.all_gather(weight, 'fsdp', axis=0, tiled=True)  73.6 us
    dot_general x1, matrix products, per_device(): values = jnp.einsum('rpk,rpjk->rpj', coeffs, selector, precision=highest)  19 us
    unnamed x20, local copies, waits for them, and re-layouts  18.9 us
    dot_general x1, matrix products, per_device(): jnp.einsum('grpj,rpjk->grpk', every_group, selector, precision=highest)  18 us
    dot_general x1, matrix products, per_device(): jnp.einsum('rpj,rpjk->rpk', values, selector, precision=highest)  15.8 us
  transfers between devices with their start and end apart: 3, of which 2 were waited for; matrix products, arithmetic and copies ran while one was open for 15% of the time, Pallas kernels for 0%

commit v1 on v0

v1 whole, which is shorter than its diff:
```python
import functools

import jax
import jax.numpy as jnp
import numpy as np
from jax import lax
from jax.experimental import pallas as pl
from jax.experimental.pallas import tpu as pltpu
from jax.sharding import Mesh, PartitionSpec as P

PIECE = 64
TOPK = 16
FREQ = 32
SLOT = 256
GROUP = 128 // FREQ * PIECE

BF16 = jnp.bfloat16
F32 = jnp.float32
HIGHEST = lax.Precision.HIGHEST
VMEM = pl.BlockSpec(memory_space=pltpu.VMEM)
SMEM = pl.BlockSpec(memory_space=pltpu.SMEM)
ANY = pl.BlockSpec(memory_space=pl.ANY)
PARAMS = pltpu.CompilerParams(vmem_limit_bytes=40 * 1024 * 1024)


def group_table():
    k = np.arange(FREQ)[:, None].astype(np.float64)
    n = np.arange(PIECE)[None, :].astype(np.float64)
    scale = np.where(k == 0, np.sqrt(1.0 / PIECE), np.sqrt(2.0 / PIECE))
    rows = scale * np.cos(np.pi * (2 * n + 1) * k / (2 * PIECE))
    return jnp.asarray(np.kron(np.eye(GROUP // PIECE), rows.T), F32)


def spread_table(pieces):
    table = np.zeros((TOPK, pieces * TOPK, pieces * FREQ), np.float32)
    for j in range(TOPK):
        for p in range(pieces):
            table[j, p * TOPK + j, p * FREQ : (p + 1) * FREQ] = 1.0
    return jnp.asarray(table, BF16)


def split_kernel(y_ref, tok_ref, *rest):
    outs, sems = rest[:-1], rest[-1]
    width = outs[0].shape[1]
    copies = []
    for d, out in enumerate(outs):
        start = pl.multiple_of(lax.bitwise_xor(y_ref[0], d) * width, width)
        copies.append(pltpu.make_async_copy(tok_ref.at[:, pl.ds(start, width)], out, sems.at[d]))
    for copy in copies:
        copy.start()
    for copy in copies:
        copy.wait()


def split_tokens(y, tokens, ny):
    rows, width = tokens.shape[0], tokens.shape[1] // ny
    return pl.pallas_call(
        split_kernel,
        out_shape=[jax.ShapeDtypeStruct((rows, width), BF16)] * ny,
        in_specs=[SMEM, ANY],
        out_specs=[ANY] * ny,
        scratch_shapes=[pltpu.SemaphoreType.DMA((ny,))],
    )(y, tokens)


def contract_rows(left, right):
    return lax.dot_general(left, right, (((0,), (0,)), ((), ())), preferred_element_type=F32)


def grad_kernel(ny, nz, z_ref, *rest):
    toks, cots = rest[:ny], rest[ny : 2 * ny]
    outs, acc = rest[2 * ny : 2 * ny + nz], rest[-1]
    acc[...] = contract_rows(toks[0][...], cots[0][...])
    for tok, cot in zip(toks[1:], cots[1:]):
        acc[...] += contract_rows(tok[...], cot[...])
    rows = outs[0].shape[0]
    for k, out in enumerate(outs):
        block = lax.rem(z_ref[0] + k, nz)
        start = pl.multiple_of(block * rows, 16)
        out[...] = acc[pl.ds(start, rows), :].astype(out.dtype)


def grad_blocks(z, toks, cots, nz):
    ny = len(toks)
    depth, width = toks[0].shape[1], cots[0].shape[1]
    rows = depth // nz
    return pl.pallas_call(
        functools.partial(grad_kernel, ny, nz),
        out_shape=[jax.ShapeDtypeStruct((rows, width), F32 if k == 0 else BF16) for k in range(nz)],
        in_specs=[SMEM] + [VMEM] * (2 * ny),
        out_specs=[VMEM] * nz,
        scratch_shapes=[pltpu.VMEM((depth, width), F32)],
        compiler_params=PARAMS,
    )(z, *toks, *cots)


def keep_kernel(kept_ref, spread_ref, keep_ref):
    kept = kept_ref[...].astype(F32).astype(BF16)
    shape = keep_ref.shape
    freq = lax.rem(lax.broadcasted_iota(jnp.int32, shape, 1), FREQ).astype(F32)
    keep = jnp.zeros(shape, F32)
    for j in range(TOPK):
        index = jnp.dot(kept, spread_ref[j], preferred_element_type=F32)
        keep = jnp.where(index == freq, 1.0, keep)
    keep_ref[...] = keep


def keep_mask(kept_index):
    rows, slots = kept_index.shape
    pieces = slots // TOPK
    return pl.pallas_call(
        keep_kernel,
        out_shape=jax.ShapeDtypeStruct((rows, pieces * FREQ), F32),
        in_specs=[VMEM] * 2,
        out_specs=VMEM,
        compiler_params=PARAMS,
    )(kept_index, spread_table(pieces))


def encode_kernel(momentum_ref, keep_ref, table_ref, table_t_ref, own_ref, *rest):
    parts, (new_ref, coeff_ref) = rest[:-2], rest[-2:]
    width = parts[0].shape[1]
    halves = momentum_ref.shape[1] // width
    for h in range(halves):
        cols = slice(h * width, (h + 1) * width)
        grad = own_ref[:, cols]
        for part in parts[h::halves]:
            grad = grad + part[...].astype(F32)
        new_ref[:, cols] = 0.9 * momentum_ref[:, cols] + grad
    for g in range(momentum_ref.shape[1] // GROUP):
        cols = slice(g * GROUP, (g + 1) * GROUP)
        lanes = slice(g * 128, (g + 1) * 128)
        blended = new_ref[:, cols]
        coeffs = jnp.dot(blended, table_ref[...], precision=HIGHEST, preferred_element_type=F32)
        coeffs = coeffs * keep_ref[:, lanes]
        coeff_ref[:, lanes] = coeffs.astype(BF16)
        rebuilt = jnp.dot(coeffs, table_t_ref[...], precision=HIGHEST, preferred_element_type=F32)
        new_ref[:, cols] = blended - rebuilt


def encode(momentum, keep, table, own, parts):
    return pl.pallas_call(
        encode_kernel,
        out_shape=[
            jax.ShapeDtypeStruct(momentum.shape, F32),
            jax.ShapeDtypeStruct(keep.shape, BF16),
        ],
        in_specs=[VMEM] * (5 + len(parts)),
        out_specs=[VMEM] * 2,
        compiler_params=PARAMS,
    )(momentum, keep, table, table.T, own, *parts)


def decode_kernel(mine_ref, other_ref, table_t_ref, update_ref):
    for g in range(update_ref.shape[1] // GROUP):
        lanes = slice(g * 128, (g + 1) * 128)
        coeffs = mine_ref[:, lanes] + other_ref[:, lanes]
        update_ref[:, g * GROUP : (g + 1) * GROUP] = jnp.dot(
            coeffs, table_t_ref[...], precision=HIGHEST, preferred_element_type=F32
        )


def decode(mine, other, table, width):
    return pl.pallas_call(
        decode_kernel,
        out_shape=jax.ShapeDtypeStruct((mine.shape[0], width), F32),
        in_specs=[VMEM] * 3,
        out_specs=VMEM,
        compiler_params=PARAMS,
    )(mine, other, table.T)


def swap(array, axis, d):
    return lax.ppermute(array, axis, [(i, i ^ d) for i in range(lax.axis_size(axis))])


def shift(array, axis, d):
    size = lax.axis_size(axis)
    return lax.ppermute(array, axis, [(i, (i + d) % size) for i in range(size)])


def reduce_ring(blocks):
    nz = len(blocks)
    width = blocks[0].shape[1] // 2
    parts = []
    for sign in (1, -1):
        for h in range(2):
            cols = slice(h * width, (h + 1) * width)
            far = nz // 2 if (sign == 1) == (h == 0) else nz // 2 - 1
            moving = blocks[sign * far % nz][:, cols]
            for k in range(far - 1, -1, -1):
                moving = shift(moving, "z", sign)
                if k:
                    own = blocks[sign * k % nz][:, cols]
                    moving = (moving.astype(F32) + own.astype(F32)).astype(BF16)
            parts.append(moving)
    return parts


def per_device(tokens, cotangent, weight, momentum, lengths, kept_index):
    ny, nz = lax.axis_size("y"), lax.axis_size("z")
    y = lax.axis_index("y").astype(jnp.int32).reshape(1)
    z = lax.axis_index("z").astype(jnp.int32).reshape(1)
    core = lax.axis_index("core")
    width = weight.shape[1]
    half = width // 2

    weight_half = lax.dynamic_slice_in_dim(weight, core * half, half, axis=1)
    weight_mine = lax.all_gather(weight_half, "z", axis=0, tiled=True)

    live = lax.broadcasted_iota(jnp.int32, (lengths.shape[0], SLOT), 1) < lengths[:, None]
    masked = cotangent * live.reshape(-1, 1).astype(BF16)
    toks = split_tokens(y, tokens, ny)
    toks = [toks[0]] + [swap(toks[d], "y", d) for d in range(1, ny)]
    cots = [masked] + [swap(masked, "y", d) for d in range(1, ny)]

    weight_other = swap(weight_mine, "core", 1)
    weight_quarter = jnp.where(
        core == 0,
        jnp.concatenate([weight_mine, weight_other], axis=1),
        jnp.concatenate([weight_other, weight_mine], axis=1),
    )

    blocks = grad_blocks(z, toks, cots, nz)
    parts = reduce_ring(blocks)

    total = jnp.dot(toks[0], weight_quarter, preferred_element_type=F32)
    sent = [jnp.dot(toks[d], weight_quarter, preferred_element_type=F32).astype(BF16) for d in range(1, ny)]
    for d in range(1, ny):
        total = total + swap(sent[d - 1], "y", d).astype(F32)
    projected = total.astype(BF16)

    table = group_table()
    keep = keep_mask(kept_index)
    new_momentum, coeffs = encode(momentum[0], keep, table, blocks[0], parts)
    one, two, three = (swap(coeffs, "x", d).astype(F32) for d in (1, 2, 3))
    mine = (coeffs.astype(F32) + one) + (two + three)
    other = swap(mine, "core", 1)
    update = decode(mine, other, table, width)
    return (projected, new_momentum[None], update)


def solution(mesh):
    fine = Mesh(mesh.devices.reshape(4, 2, 4, 8), ("x", "core", "y", "z"))
    rep, fsdp = ("x", "core"), ("y", "z")
    placed = (
        P(rep + fsdp, None),
        P(rep + fsdp, None),
        P(fsdp, None),
        P(rep, fsdp, None),
        P(rep + fsdp),
        P(fsdp, None),
    )
    return jax.shard_map(
        per_device,
        mesh=fine,
        in_specs=placed,
        out_specs=(P(rep + fsdp, None), P(rep, fsdp, None), P(fsdp, None)),
        check_vma=False,
    )
```

time: 453 us -> 237 us (0.52)
  waiting for transfers between devices: 302 us -> 70.7 us
  Pallas kernels: 0 us -> 81.4 us
  matrix products: 75.1 us -> 11 us
  local copies, waits for them, and re-layouts: 58 us -> 9.8 us
  starting transfers between devices: 0.12 us -> 40.9 us
    unnamed x4 -> x1, waiting for transfers between devices: 228 us -> 0.02 us
    pallas_call x0 -> x5, Pallas kernels: none -> 81.4 us  [the longest x1 72.6 us: split_tokens(): pl.pallas_call(split_kernel, out_shape=[jax.ShapeDtypeStruct((rows, width...]
    all_gather x2 -> x1, waiting for transfers between devices: 73.6 us -> 0.01 us  [per_device(): weight_mine = lax.all_gather(weight_half, 'z', axis=0, tiled=True)]
    ppermute x0 -> x28, waiting for transfers between devices: none -> 70.7 us  [the longest x14 60.3 us: swap(): lax.ppermute(array, axis, [(i, i ^ d) for i in range(lax.axis_size(axis))])]
    dot_general x8 -> x4, matrix products: 75.1 us -> 11 us  [the longest x3 7.56 us: per_device(): jnp.dot(toks[d], weight_quarter, preferred_element_type=F32).astype(BF16)]
    ppermute x0 -> x28, starting transfers between devices: none -> 40.8 us  [the longest x14 26 us: swap(): lax.ppermute(array, axis, [(i, i ^ d) for i in range(lax.axis_size(axis))])]
    reshape x7 -> x0, local copies, waits for them, and re-layouts: 23.2 us -> none  [the longest x1 8.89 us: per_device(): dense_every.reshape(num_rep, local_rows, pairs, 128)]
    unnamed x20 -> x34, local copies, waits for them, and re-layouts: 18.9 us -> 7.12 us
  transfers between devices with their start and end apart: 3 -> 29, of which waited for: 2 -> 11; matrix products, arithmetic and copies ran while one was open for 15% -> 7% of each run, Pallas kernels for 0% -> 35%
where the time goes in v1:
time: 237 us; the launch traced here: 234 us
  Pallas kernels  81.4 us (34%)
  waiting for transfers between devices  70.7 us (30%)
  starting transfers between devices  40.9 us (17%)
  between operations  14.9 us (6%)
  matrix products  11 us (5%)
  local copies, waits for them, and re-layouts  9.8 us (4%)
  other arithmetic  5.74 us (2%)
    pallas_call x1, Pallas kernels, split_tokens(): pl.pallas_call(split_kernel, out_shape=[jax.ShapeDtypeStruct((rows, width...  72.6 us
    ppermute x14, waiting for transfers between devices, swap(): lax.ppermute(array, axis, [(i, i ^ d) for i in range(lax.axis_size(axis))])  60.3 us
    ppermute x14, starting transfers between devices, swap(): lax.ppermute(array, axis, [(i, i ^ d) for i in range(lax.axis_size(axis))])  26 us
    ppermute x14, starting transfers between devices, shift(): return lax.ppermute(array, axis, [(i, (i + d) % size) for i in range(size)])  14.9 us
    ppermute x14, waiting for transfers between devices, shift(): return lax.ppermute(array, axis, [(i, (i + d) % size) for i in range(size)])  10.4 us
    dot_general x3, matrix products, per_device(): jnp.dot(toks[d], weight_quarter, preferred_element_type=F32).astype(BF16)  7.56 us
    unnamed x34, local copies, waits for them, and re-layouts  7.12 us
  transfers between devices with their start and end apart: 29, of which 11 were waited for; matrix products, arithmetic and copies ran while one was open for 7% of the time, Pallas kernels for 35%

profile of v1, /device:TPU:1, one launch (start us, length us, event | category | flops | bytes accessed | tf_op | source)
XLA Modules:
  0.0 234.5 jit_solution(14738893329282838816)
XLA Ops:
  10.6 2.2 collective-permute-start.7
  12.8 72.6 %shard_map.103 = (bf16[256,1152]{1,0:T(8,128)(2,1)}, bf16[256,1152]{1,0:T(8,128)(2,1)}, bf16[256,1152]{1,0:T(8,128)(2,1)}, bf16[256,1152]{1,0:T(8,128)(2,1)}) custom-call(s32[1]{0:T(128)} %bitcast.y_ref, bf16[256,4608]{1,0:T(8,128)(2,1)} %tok_ref.1), custom_call_target="tpu_custom_call" | custom-call | tf_op jit(solution)/shard_map/pallas_call | solution.py:57
  85.6 3.1 %collective-permute-start.3 = (bf16[256,1152]{1,0:T(8,128)(2,1)}, bf16[256,1152]{1,0:T(8,128)(2,1)S(1)}, u32[]{:S(2)}, u32[]{:S(2)}) collective-permute-start(bf16[256,1152]{1,0:T(8,128)(2,1)} %get-tuple-element.19), channel_id=1, source_target_pairs={{0,16},{8,24},{16,0},{24,8},{1,17},{9,25},{17,1},{25,9},{2,18},{10... | collective-permute-start | bytes 1769480 | tf_op jit(solution)/shard_map/ppermute | solution.py:174
  91.4 33.8 %collective-permute-done.8.rest_6_ = bf16[256,1024]{1,0:T(8,128)(2,1)} collective-permute-done((bf16[256,1024]{1,0:T(8,128)(2,1)S(1)}, bf16[256,1024]{1,0:T(8,128)(2,1)}, u32[]{:S(2)}, u32[]{:S(2)}) %collective-permute-start.8) | collective-permute-done | bytes 524320 | tf_op jit(solution)/shard_map/ppermute | solution.py:174
  125.3 13.3 %collective-permute-done.9.rest_7_ = bf16[256,1024]{1,0:T(8,128)(2,1)} collective-permute-done((bf16[256,1024]{1,0:T(8,128)(2,1)S(1)}, bf16[256,1024]{1,0:T(8,128)(2,1)}, u32[]{:S(2)}, u32[]{:S(2)}) %collective-permute-start.9) | collective-permute-done | bytes 524320 | tf_op jit(solution)/shard_map/ppermute | solution.py:174
  139.6 4.1 %shard_map.105 = (f32[144,1024]{1,0:T(8,128)S(1)}, bf16[144,1024]{1,0:T(8,128)(2,1)S(1)}, bf16[144,1024]{1,0:T(8,128)(2,1)S(1)}, bf16[144,1024]{1,0:T(8,128)(2,1...) custom-call(s32[1]{0:T(128)} %bitcast.2.z_ref, ...), custom_call_target="tpu_custom_call" | custom-call | tf_op jit(solution)/shard_map/pallas_call | solution.py:87
  147.4 5.6 %collective-permute-start.20 = (bf16[144,512]{1,0:T(8,128)(2,1)S(1)}, bf16[144,512]{1,0:T(8,128)(2,1)S(1)}, u32[]{:S(2)}, u32[]{:S(2)}) collective-permute-start(bf16[144,512]{1,0:T(8,128)(2,1)S(1)} %get-tuple-element.35), channel_id=1, source_target_pairs={{0,7},{1,0},{2,1},{3,2},{4,3},{5,4},{6,5},{7,6},{8,15},{9,8},{10,9... | collective-permute-start | bytes 442376 | tf_op jit(solution)/shard_map/ppermute | solution.py:179
  156.5 2.7 %collective-permute-start.21 = (bf16[144,512]{1,0:T(8,128)(2,1)}, bf16[144,512]{1,0:T(8,128)(2,1)}, u32[]{:S(2)}, u32[]{:S(2)}) collective-permute-start(bf16[144,512]{1,0:T(8,128)(2,1)} %add_convert_fusion.2), channel_id=1, source_target_pairs={{0,7},{1,0},{2,1},{3,2},{4,3},{5,4},{6,5},{7,6},{8,15},{9,8},{10,9... | collective-permute-start | bytes 442376 | tf_op jit(solution)/shard_map/ppermute | solution.py:179
  159.1 3.9 %collective-permute-start = (bf16[1152,512]{1,0:T(8,128)(2,1)}, bf16[1152,512]{1,0:T(8,128)(2,1)}, u32[]{:S(2)}, u32[]{:S(2)}) collective-permute-start(bf16[1152,512]{1,0:T(8,128)(2,1)} %all-gather.2.cloned.1.call-done), channel_id=1, source_target_pairs={{0,32},{32,0},{1,33},{33,1},{2,34},{34,2},{3,35},{35,3},{4,36},{36... | collective-permute-start | bytes 3538952 | tf_op jit(solution)/shard_map/ppermute | solution.py:174
  165.3 2.9 %collective-permute-start.18 = (bf16[144,512]{1,0:T(8,128)(2,1)S(1)}, bf16[144,512]{1,0:T(8,128)(2,1)S(1)}, u32[]{:S(2)}, u32[]{:S(2)}) collective-permute-start(bf16[144,512]{1,0:T(8,128)(2,1)S(1)} %get-tuple-element.34), channel_id=1, source_target_pairs={{0,7},{1,0},{2,1},{3,2},{4,3},{5,4},{6,5},{7,6},{8,15},{9,8},{10,9... | collective-permute-start | bytes 442376 | tf_op jit(solution)/shard_map/ppermute | solution.py:179
  170.3 3.1 %collective-permute-done.22 = bf16[144,512]{1,0:T(8,128)(2,1)S(1)} collective-permute-done((bf16[144,512]{1,0:T(8,128)(2,1)S(1)}, bf16[144,512]{1,0:T(8,128)(2,1)S(1)}, u32[]{:S(2)}, u32[]{:S(2)}) %collective-permute-start.22) | collective-permute-done | bytes 147488 | tf_op jit(solution)/shard_map/ppermute | solution.py:179
  178.5 2.2 copy-done.1
  181.5 2.4 %collective-permute-done.13.rest_0_ = bf16[144,512]{1,0:T(8,128)(2,1)S(1)} collective-permute-done((bf16[144,512]{1,0:T(8,128)(2,1)}, bf16[144,512]{1,0:T(8,128)(2,1)S(1)}, u32[]{:S(2)}, u32[]{:S(2)}) %collective-permute-start.13) | collective-permute-done | bytes 147488 | tf_op jit(solution)/shard_map/ppermute | solution.py:179
  185.5 2.5 %shard_map.106 = (f32[144,1024]{1,0:T(8,128)}, bf16[144,512]{1,0:T(8,128)(2,1)S(1)}) custom-call(f32[144,1024]{1,0:T(8,128)S(1)} %bitcast.10, f32[144,512]{1,0:T(8,128)S(1)} %shard_map.104.keep_ref, f32[256,128]{1,0:T(8,128)S(1)} %copy-done.15, f32[128,256]{1,0:T(8,128)S(1)} %copy-done.7, f32[144,1024]{1,0:T(8,128)S(1)} %copy-done.6, ...), custom_call_target="tpu_custom_call" | custom-call | tf_op jit(solution)/shard_map/pallas_call | solution.py:142
  189.2 2.5 %collective-permute-start.25 = (bf16[144,512]{1,0:T(8,128)(2,1)S(1)}, bf16[144,512]{1,0:T(8,128)(2,1)S(1)}, u32[]{:S(2)}, u32[]{:S(2)}) collective-permute-start(bf16[144,512]{1,0:T(8,128)(2,1)S(1)} %get-tuple-element.30), channel_id=1, source_target_pairs={{0,128},{64,192},{128,0},{192,64},{1,129},{65,193},{129,1},{193,65... | collective-permute-start | bytes 442376 | tf_op jit(solution)/shard_map/ppermute | solution.py:174
  191.9 2.5 %convolution_convert_fusion.2 = bf16[256,1024]{1,0:T(8,128)(2,1)S(1)} fusion(bf16[256,1152]{1,0:T(8,128)(2,1)S(1)} %collective-permute-done.1.rest_1_, bf16[1152,512]{1,0:T(8,128)(2,1)} %collective-permute-done, bf16[1152,512]{1,0:T(8,128)(2,1)S(1)} %copy-done.16, pred[]{:T(512)S(6)} %eq.3), kind=kOutput, calls=%fused_computation.6 | convolution fusion | flops 614858752 | bytes 3473409 | tf_op jit(solution)/shard_map/dot_general | solution.py:228
  194.5 2.5 %convolution_convert_fusion.1 = bf16[256,1024]{1,0:T(8,128)(2,1)S(1)} fusion(bf16[256,1152]{1,0:T(8,128)(2,1)S(1)} %collective-permute-done.3.rest_2_, bf16[1152,512]{1,0:T(8,128)(2,1)} %collective-permute-done, bf16[1152,512]{1,0:T(8,128)(2,1)S(1)} %copy-done.16, pred[]{:T(512)S(6)} %eq.3), kind=kOutput, calls=%fused_computation.5 | convolution fusion | flops 614858752 | bytes 3473409 | tf_op jit(solution)/shard_map/dot_general | solution.py:228
  197.0 2.2 collective-permute-start.4
  199.3 2.5 %convolution_convert_fusion = bf16[256,1024]{1,0:T(8,128)(2,1)S(1)} fusion(bf16[256,1152]{1,0:T(8,128)(2,1)S(1)} %collective-permute-done.5.rest_3_, bf16[1152,512]{1,0:T(8,128)(2,1)} %collective-permute-done, bf16[1152,512]{1,0:T(8,128)(2,1)S(1)} %copy-done.16, pred[]{:T(512)S(6)} %eq.3), kind=kOutput, calls=%fused_computation.4 | convolution fusion | flops 614858752 | bytes 3473409 | tf_op jit(solution)/shard_map/dot_general | solution.py:228
  201.8 2.0 collective-permute-start.6
  203.9 5.7 %collective-permute-start.27 = (f32[144,512]{1,0:T(8,128)S(1)}, f32[144,512]{1,0:T(8,128)S(1)}, u32[]{:S(2)}, u32[]{:S(2)}) collective-permute-start(f32[144,512]{1,0:T(8,128)S(1)} %add_add_fusion.mine_ref), channel_id=1, source_target_pairs={{0,32},{32,0},{1,33},{33,1},{2,34},{34,2},{3,35},{35,3},{4,36},{36... | collective-permute-start | bytes 884744 | tf_op jit(solution)/shard_map/ppermute | solution.py:174
  212.3 2.5 %collective-permute-done.4 = bf16[256,1024]{1,0:T(8,128)(2,1)S(1)} collective-permute-done((bf16[256,1024]{1,0:T(8,128)(2,1)S(1)}, bf16[256,1024]{1,0:T(8,128)(2,1)S(1)}, u32[]{:S(2)}, u32[]{:S(2)}) %collective-permute-start.4) | collective-permute-done | bytes 524320 | tf_op jit(solution)/shard_map/ppermute | solution.py:174
  214.8 9.4 %collective-permute-done.6 = bf16[256,1024]{1,0:T(8,128)(2,1)S(1)} collective-permute-done((bf16[256,1024]{1,0:T(8,128)(2,1)S(1)}, bf16[256,1024]{1,0:T(8,128)(2,1)S(1)}, u32[]{:S(2)}, u32[]{:S(2)}) %collective-permute-start.6) | collective-permute-done | bytes 524320 | tf_op jit(solution)/shard_map/ppermute | solution.py:174
  224.2 3.5 %fusion.2 = bf16[256,1024]{1,0:T(8,128)(2,1)} fusion(bf16[256,1152]{1,0:T(8,128)(2,1)S(1)} %copy-done.3, bf16[256,1024]{1,0:T(8,128)(2,1)S(1)} %collective-permute-done.6, bf16[256,1024]{1,0:T(8,128)(2,1)S(1)} %collective-permute-done.4, bf16[256,1024]{1,0:T(8,128)(2,1)S(1)} %collective-permute-done.2, bf16[1152,512]{1,0:T(8,128)(2,1)} %collective-permute-done, ...), kind=kOutput, calls=%fused_computation.7 | convolution fusion | flops 616431616 | bytes 5046273 | tf_op jit(solution)/shard_map/dot_general | solution.py:227
  (91 shorter events, 29.9 us)
Async XLA Ops:
  7.2 152.0 %all-gather.2.cloned.1.call-start = ((), (), s32[]{:S(2)}) async-start(), calls=%async_computation | async-start | bytes 1327104 | tf_op jit(solution)/shard_map/all_gather | solution.py:209
  10.6 80.2 %collective-permute-start.7 = (bf16[256,1024]{1,0:T(8,128)(2,1)S(1)}, bf16[256,1024]{1,0:T(8,128)(2,1)S(1)}, u32[]{:S(2)}, u32[]{:S(2)}) collective-permute-start(bf16[256,1024]{1,0:T(8,128)(2,1)S(1)} %broadcast_multiply_fusion.rest_4_), channel_id=1, source_target_pairs={{0,8},{8,0},{16,24},{24,16},{1,9},{9,1},{17,25},{25,17},{2,10},{10... | collective-permute-start | bytes 1572872 | tf_op jit(solution)/shard_map/ppermute | solution.py:174
  85.5 53.1 %collective-permute-start.1 = (bf16[256,1152]{1,0:T(8,128)(2,1)}, bf16[256,1152]{1,0:T(8,128)(2,1)S(1)}, u32[]{:S(2)}, u32[]{:S(2)}) collective-permute-start(bf16[256,1152]{1,0:T(8,128)(2,1)} %get-tuple-element.18), channel_id=1, source_target_pairs={{0,8},{8,0},{16,24},{24,16},{1,9},{9,1},{17,25},{25,17},{2,10},{10... | collective-permute-start | bytes 1769480 | tf_op jit(solution)/shard_map/ppermute | solution.py:174
  85.6 53.0 %collective-permute-start.3 = (bf16[256,1152]{1,0:T(8,128)(2,1)}, bf16[256,1152]{1,0:T(8,128)(2,1)S(1)}, u32[]{:S(2)}, u32[]{:S(2)}) collective-permute-start(bf16[256,1152]{1,0:T(8,128)(2,1)} %get-tuple-element.19), channel_id=1, source_target_pairs={{0,16},{8,24},{16,0},{24,8},{1,17},{9,25},{17,1},{25,9},{2,18},{10... | collective-permute-start | bytes 1769480 | tf_op jit(solution)/shard_map/ppermute | solution.py:174
  88.6 49.9 %collective-permute-start.5 = (bf16[256,1152]{1,0:T(8,128)(2,1)}, bf16[256,1152]{1,0:T(8,128)(2,1)S(1)}, u32[]{:S(2)}, u32[]{:S(2)}) collective-permute-start(bf16[256,1152]{1,0:T(8,128)(2,1)} %get-tuple-element.20), channel_id=1, source_target_pairs={{0,24},{8,16},{16,8},{24,0},{1,25},{9,17},{17,9},{25,1},{2,26},{10... | collective-permute-start | bytes 1769480 | tf_op jit(solution)/shard_map/ppermute | solution.py:174
  89.4 35.9 %collective-permute-start.8 = (bf16[256,1024]{1,0:T(8,128)(2,1)S(1)}, bf16[256,1024]{1,0:T(8,128)(2,1)}, u32[]{:S(2)}, u32[]{:S(2)}) collective-permute-start(bf16[256,1024]{1,0:T(8,128)(2,1)S(1)} %broadcast_multiply_fusion.rest_4_), channel_id=1, source_target_pairs={{0,16},{8,24},{16,0},{24,8},{1,17},{9,25},{17,1},{25,9},{2,18},{10... | collective-permute-start | bytes 1572872 | tf_op jit(solution)/shard_map/ppermute | solution.py:174
  90.8 47.8 %collective-permute-start.9 = (bf16[256,1024]{1,0:T(8,128)(2,1)S(1)}, bf16[256,1024]{1,0:T(8,128)(2,1)}, u32[]{:S(2)}, u32[]{:S(2)}) collective-permute-start(bf16[256,1024]{1,0:T(8,128)(2,1)S(1)} %broadcast_multiply_fusion.rest_4_), channel_id=1, source_target_pairs={{0,24},{8,16},{16,8},{24,0},{1,25},{9,17},{17,9},{25,1},{2,26},{10... | collective-permute-start | bytes 1572872 | tf_op jit(solution)/shard_map/ppermute | solution.py:174
  147.4 8.4 %collective-permute-start.20 = (bf16[144,512]{1,0:T(8,128)(2,1)S(1)}, bf16[144,512]{1,0:T(8,128)(2,1)S(1)}, u32[]{:S(2)}, u32[]{:S(2)}) collective-permute-start(bf16[144,512]{1,0:T(8,128)(2,1)S(1)} %get-tuple-element.35), channel_id=1, source_target_pairs={{0,7},{1,0},{2,1},{3,2},{4,3},{5,4},{6,5},{7,6},{8,15},{9,8},{10,9... | collective-permute-start | bytes 442376 | tf_op jit(solution)/shard_map/ppermute | solution.py:179
  153.6 10.5 %collective-permute-start.17 = (bf16[144,512]{1,0:T(8,128)(2,1)}, bf16[144,512]{1,0:T(8,128)(2,1)S(1)}, u32[]{:S(2)}, u32[]{:S(2)}) collective-permute-start(bf16[144,512]{1,0:T(8,128)(2,1)} %slice.49), channel_id=1, source_target_pairs={{0,7},{1,0},{2,1},{3,2},{4,3},{5,4},{6,5},{7,6},{8,15},{9,8},{10,9... | collective-permute-start | bytes 442376 | tf_op jit(solution)/shard_map/ppermute | solution.py:179
  154.3 8.7 %collective-permute-start.10 = (bf16[144,512]{1,0:T(8,128)(2,1)}, bf16[144,512]{1,0:T(8,128)(2,1)}, u32[]{:S(2)}, u32[]{:S(2)}) collective-permute-start(bf16[144,512]{1,0:T(8,128)(2,1)} %get-tuple-element.36), channel_id=1, source_target_pairs={{0,1},{1,2},{2,3},{3,4},{4,5},{5,6},{6,7},{7,0},{8,9},{9,10},{10,1... | collective-permute-start | bytes 442376 | tf_op jit(solution)/shard_map/ppermute | solution.py:179
  155.7 12.5 %collective-permute-start.14 = (bf16[144,512]{1,0:T(8,128)(2,1)}, bf16[144,512]{1,0:T(8,128)(2,1)S(1)}, u32[]{:S(2)}, u32[]{:S(2)}) collective-permute-start(bf16[144,512]{1,0:T(8,128)(2,1)} %slice.46), channel_id=1, source_target_pairs={{0,1},{1,2},{2,3},{3,4},{4,5},{5,6},{6,7},{7,0},{8,9},{9,10},{10,1... | collective-permute-start | bytes 442376 | tf_op jit(solution)/shard_map/ppermute | solution.py:179
  156.5 7.7 %collective-permute-start.21 = (bf16[144,512]{1,0:T(8,128)(2,1)}, bf16[144,512]{1,0:T(8,128)(2,1)}, u32[]{:S(2)}, u32[]{:S(2)}) collective-permute-start(bf16[144,512]{1,0:T(8,128)(2,1)} %add_convert_fusion.2), channel_id=1, source_target_pairs={{0,7},{1,0},{2,1},{3,2},{4,3},{5,4},{6,5},{7,6},{8,15},{9,8},{10,9... | collective-permute-start | bytes 442376 | tf_op jit(solution)/shard_map/ppermute | solution.py:179
  159.1 32.7 %collective-permute-start = (bf16[1152,512]{1,0:T(8,128)(2,1)}, bf16[1152,512]{1,0:T(8,128)(2,1)}, u32[]{:S(2)}, u32[]{:S(2)}) collective-permute-start(bf16[1152,512]{1,0:T(8,128)(2,1)} %all-gather.2.cloned.1.call-done), channel_id=1, source_target_pairs={{0,32},{32,0},{1,33},{33,1},{2,34},{34,2},{3,35},{35,3},{4,36},{36... | collective-permute-start | bytes 3538952 | tf_op jit(solution)/shard_map/ppermute | solution.py:174
  169.8 6.4 %collective-permute-start.12 = (bf16[144,512]{1,0:T(8,128)(2,1)S(1)}, bf16[144,512]{1,0:T(8,128)(2,1)S(1)}, u32[]{:S(2)}, u32[]{:S(2)}) collective-permute-start(bf16[144,512]{1,0:T(8,128)(2,1)S(1)} %get-tuple-element.40), channel_id=1, source_target_pairs={{0,1},{1,2},{2,3},{3,4},{4,5},{5,6},{6,7},{7,0},{8,9},{9,10},{10,1... | collective-permute-start | bytes 442376 | tf_op jit(solution)/shard_map/ppermute | solution.py:179
  169.9 7.8 %collective-permute-start.15 = (bf16[144,512]{1,0:T(8,128)(2,1)S(1)}, bf16[144,512]{1,0:T(8,128)(2,1)S(1)}, u32[]{:S(2)}, u32[]{:S(2)}) collective-permute-start(bf16[144,512]{1,0:T(8,128)(2,1)S(1)} %get-tuple-element.39), channel_id=1, source_target_pairs={{0,1},{1,2},{2,3},{3,4},{4,5},{5,6},{6,7},{7,0},{8,9},{9,10},{10,1... | collective-permute-start | bytes 442376 | tf_op jit(solution)/shard_map/ppermute | solution.py:179
  174.2 7.2 %collective-permute-start.19 = (bf16[144,512]{1,0:T(8,128)(2,1)}, bf16[144,512]{1,0:T(8,128)(2,1)S(1)}, u32[]{:S(2)}, u32[]{:S(2)}) collective-permute-start(bf16[144,512]{1,0:T(8,128)(2,1)} %get-tuple-element.32), channel_id=1, source_target_pairs={{0,7},{1,0},{2,1},{3,2},{4,3},{5,4},{6,5},{7,6},{8,15},{9,8},{10,9... | collective-permute-start | bytes 442376 | tf_op jit(solution)/shard_map/ppermute | solution.py:179
  178.5 7.0 %collective-permute-start.16 = (bf16[144,512]{1,0:T(8,128)(2,1)}, bf16[144,512]{1,0:T(8,128)(2,1)S(1)}, u32[]{:S(2)}, u32[]{:S(2)}) collective-permute-start(bf16[144,512]{1,0:T(8,128)(2,1)} %get-tuple-element.37), channel_id=1, source_target_pairs={{0,1},{1,2},{2,3},{3,4},{4,5},{5,6},{6,7},{7,0},{8,9},{9,10},{10,1... | collective-permute-start | bytes 442376 | tf_op jit(solution)/shard_map/ppermute | solution.py:179
  188.0 13.8 %collective-permute-start.24 = (bf16[144,512]{1,0:T(8,128)(2,1)S(1)}, bf16[144,512]{1,0:T(8,128)(2,1)S(1)}, u32[]{:S(2)}, u32[]{:S(2)}) collective-permute-start(bf16[144,512]{1,0:T(8,128)(2,1)S(1)} %get-tuple-element.30), channel_id=1, source_target_pairs={{0,64},{64,0},{128,192},{192,128},{1,65},{65,1},{129,193},{193,129... | collective-permute-start | bytes 442376 | tf_op jit(solution)/shard_map/ppermute | solution.py:174
  189.2 14.6 %collective-permute-start.25 = (bf16[144,512]{1,0:T(8,128)(2,1)S(1)}, bf16[144,512]{1,0:T(8,128)(2,1)S(1)}, u32[]{:S(2)}, u32[]{:S(2)}) collective-permute-start(bf16[144,512]{1,0:T(8,128)(2,1)S(1)} %get-tuple-element.30), channel_id=1, source_target_pairs={{0,128},{64,192},{128,0},{192,64},{1,129},{65,193},{129,1},{193,65... | collective-permute-start | bytes 442376 | tf_op jit(solution)/shard_map/ppermute | solution.py:174
  191.7 12.1 %collective-permute-start.26 = (bf16[144,512]{1,0:T(8,128)(2,1)S(1)}, bf16[144,512]{1,0:T(8,128)(2,1)S(1)}, u32[]{:S(2)}, u32[]{:S(2)}) collective-permute-start(bf16[144,512]{1,0:T(8,128)(2,1)S(1)} %get-tuple-element.30), channel_id=1, source_target_pairs={{0,192},{64,128},{128,64},{192,0},{1,193},{65,129},{129,65},{193,1... | collective-permute-start | bytes 442376 | tf_op jit(solution)/shard_map/ppermute | solution.py:174
  194.4 17.9 %collective-permute-start.2 = (bf16[256,1024]{1,0:T(8,128)(2,1)S(1)}, bf16[256,1024]{1,0:T(8,128)(2,1)S(1)}, u32[]{:S(2)}, u32[]{:S(2)}) collective-permute-start(bf16[256,1024]{1,0:T(8,128)(2,1)S(1)} %convolution_convert_fusion.2), channel_id=1, source_target_pairs={{0,8},{8,0},{16,24},{24,16},{1,9},{9,1},{17,25},{25,17},{2,10},{10... | collective-permute-start | bytes 1572872 | tf_op jit(solution)/shard_map/ppermute | solution.py:174
  197.0 17.8 %collective-permute-start.4 = (bf16[256,1024]{1,0:T(8,128)(2,1)S(1)}, bf16[256,1024]{1,0:T(8,128)(2,1)S(1)}, u32[]{:S(2)}, u32[]{:S(2)}) collective-permute-start(bf16[256,1024]{1,0:T(8,128)(2,1)S(1)} %convolution_convert_fusion.1), channel_id=1, source_target_pairs={{0,16},{8,24},{16,0},{24,8},{1,17},{9,25},{17,1},{25,9},{2,18},{10... | collective-permute-start | bytes 1572872 | tf_op jit(solution)/shard_map/ppermute | solution.py:174
  201.8 22.4 %collective-permute-start.6 = (bf16[256,1024]{1,0:T(8,128)(2,1)S(1)}, bf16[256,1024]{1,0:T(8,128)(2,1)S(1)}, u32[]{:S(2)}, u32[]{:S(2)}) collective-permute-start(bf16[256,1024]{1,0:T(8,128)(2,1)S(1)} %convolution_convert_fusion), channel_id=1, source_target_pairs={{0,24},{8,16},{16,8},{24,0},{1,25},{9,17},{17,9},{25,1},{2,26},{10... | collective-permute-start | bytes 1572872 | tf_op jit(solution)/shard_map/ppermute | solution.py:174
  203.9 7.0 %collective-permute-start.27 = (f32[144,512]{1,0:T(8,128)S(1)}, f32[144,512]{1,0:T(8,128)S(1)}, u32[]{:S(2)}, u32[]{:S(2)}) collective-permute-start(f32[144,512]{1,0:T(8,128)S(1)} %add_add_fusion.mine_ref), channel_id=1, source_target_pairs={{0,32},{32,0},{1,33},{33,1},{2,34},{34,2},{3,35},{35,3},{4,36},{36... | collective-permute-start | bytes 884744 | tf_op jit(solution)/shard_map/ppermute | solution.py:174
  (22 other events, 178.9 us)
Sparse Core Ops, SparseCore 0:
  9.8 80.3 all-gather.1
